TPU v7x, 32 devices: a whole 2x2x4 slice. The times are simulated.
32 devices in a mesh: ctx: 16 (over z, x, core), head: 2 (over y).
Axes of the slice: x: 2, y: 2, z: 4, core: 2. Of those that a mesh axis runs over, the one named last changes fastest.
Arguments:
- queries: bfloat16 [4096, 16, 128], P(('ctx', 'head')), may hold values from -8 to 8
- keys: bfloat16 [4096, 16, 128], P(('ctx', 'head')), may hold values from -6 to 6
- values: bfloat16 [4096, 16, 128], P(('ctx', 'head')), may hold values from -6 to 6
- out_grad: bfloat16 [4096, 16, 128], P(('ctx', 'head')), may hold values from -6 to 6
- block_lists: int32 [16, 3], P('ctx'), may hold values from 0 to 15, as said below
Outputs:
- attended: bfloat16 [4096, 16, 128], P(('ctx', 'head'))
- grad_query: bfloat16 [4096, 16, 128], P(('ctx', 'head'))
- grad_key: bfloat16 [4096, 16, 128], P(('ctx', 'head'))
- grad_value: bfloat16 [4096, 16, 128], P(('ctx', 'head'))
Inputs may be any that keep to these rules, and one draw needn't show every extreme that they name: `block_lists`: row b begins with b; its other entries are distinct blocks among b - 3 to b - 1, as many of them as exist up to 2, and b again where fewer exist.
All inputs are finite; a program needn't handle non-finite values.
Results may differ from a plain program's by a relative error of at most 0.015.
Values may be sent and summed in bfloat16 or wider, within the bound.
A program may use at most 64 MiB of HBM per device.

v0:
```python
import math
import jax
import jax.numpy as jnp
from jax import lax
from jax.sharding import PartitionSpec as P

R = 3


def from_behind(block, axis, distance):
    devices = range(lax.axis_size(axis))
    route = [(i - distance, i) for i in devices if i - distance in devices]
    return lax.ppermute(block, axis, route)


def attend(query_rows, key_window, value_window, grad_rows, allowed):
    score_scale = 1.0 / math.sqrt(query_rows.shape[-1])
    scores = (
        jnp.einsum("thd,shd->hts", query_rows, key_window, preferred_element_type=jnp.float32)
        * score_scale
    )
    scores = jnp.where(allowed[None], scores, -jnp.inf)
    highest = jnp.max(scores, axis=2, keepdims=True)
    weights = jnp.exp(scores - highest)
    probability = weights / jnp.sum(weights, axis=2, keepdims=True)
    probs_low = probability.astype(jnp.bfloat16)
    attended = jnp.einsum(
        "hts,shd->thd", probs_low, value_window, preferred_element_type=jnp.float32
    ).astype(jnp.bfloat16)
    grad_probs = jnp.einsum(
        "thd,shd->hts", grad_rows, value_window, preferred_element_type=jnp.float32
    )
    centre = jnp.sum(grad_rows.astype(jnp.float32) * attended.astype(jnp.float32), axis=2).T[
        :, :, None
    ]
    grad_scores = (probability * (grad_probs - centre)).astype(jnp.bfloat16)
    grad_query = (
        jnp.einsum("hts,shd->thd", grad_scores, key_window, preferred_element_type=jnp.float32)
        * score_scale
    ).astype(jnp.bfloat16)
    key_terms = (
        jnp.einsum("hts,thd->shd", grad_scores, query_rows, preferred_element_type=jnp.float32)
        * score_scale
    )
    value_terms = jnp.einsum(
        "hts,thd->shd", probs_low, grad_rows, preferred_element_type=jnp.float32
    )
    return (attended, grad_query, key_terms, value_terms)


def block_mask(block_permitted, tile_lower_mask, length):
    row_ids = jnp.arange(length)
    lower_tri = row_ids[:, None] >= row_ids[None, :]
    allowed = block_permitted[None, :, None] & (
        (~tile_lower_mask)[None, :, None] | lower_tri[:, None, :]
    )
    return allowed.reshape(length, block_permitted.shape[0] * length)


def local(queries, keys, values, out_grad, block_lists):
    query_rows, key_rows, value_rows, grad_rows = (
        lax.all_to_all(queries, "head", split_axis=1, concat_axis=0, tiled=True),
        lax.all_to_all(keys, "head", split_axis=1, concat_axis=0, tiled=True),
        lax.all_to_all(values, "head", split_axis=1, concat_axis=0, tiled=True),
        lax.all_to_all(out_grad, "head", split_axis=1, concat_axis=0, tiled=True),
    )
    length = query_rows.shape[0]
    head_count = query_rows.shape[1]
    width = query_rows.shape[2]
    position = lax.axis_index("ctx")
    listing = block_lists[0]
    key_tiles = [key_rows]
    value_tiles = [value_rows]
    held_key, held_value = (key_rows, value_rows)
    for distance in range(1, R + 1):
        held_key, held_value = from_behind((held_key, held_value), "ctx", 1)
        key_tiles.append(held_key)
        value_tiles.append(held_value)
    offsets = jnp.arange(R + 1, dtype=jnp.int32)
    candidate_block = position - offsets
    block_permitted = jnp.any(candidate_block[:, None] == listing[None, :], axis=1) & (
        candidate_block >= 0
    )
    tile_lower_mask = offsets == 0
    key_window = jnp.concatenate(key_tiles, axis=0)
    value_window = jnp.concatenate(value_tiles, axis=0)
    count = key_window.shape[0] // length
    allowed = block_mask(block_permitted, tile_lower_mask, length)
    attended, grad_query, key_terms, value_terms = attend(
        query_rows, key_window, value_window, grad_rows, allowed
    )
    key_terms = key_terms.reshape(count, length, head_count, width)
    value_terms = value_terms.reshape(count, length, head_count, width)
    key_total = key_terms[0]
    value_total = value_terms[0]
    for distance in range(1, R + 1):
        back_key, back_value = from_behind(
            (key_terms[distance].astype(jnp.bfloat16), value_terms[distance].astype(jnp.bfloat16)),
            "ctx",
            -distance,
        )
        key_total = key_total + back_key.astype(jnp.float32)
        value_total = value_total + back_value.astype(jnp.float32)
    return (
        lax.all_to_all(attended, "head", split_axis=0, concat_axis=1, tiled=True),
        lax.all_to_all(grad_query, "head", split_axis=0, concat_axis=1, tiled=True),
        lax.all_to_all(
            key_total.astype(jnp.bfloat16), "head", split_axis=0, concat_axis=1, tiled=True
        ),
        lax.all_to_all(
            value_total.astype(jnp.bfloat16), "head", split_axis=0, concat_axis=1, tiled=True
        ),
    )


def solution(mesh):
    placed = (
        P(("ctx", "head"), None, None),
        P(("ctx", "head"), None, None),
        P(("ctx", "head"), None, None),
        P(("ctx", "head"), None, None),
        P("ctx", None),
    )
    return jax.shard_map(
        local,
        mesh=mesh,
        in_specs=placed,
        out_specs=(
            P(("ctx", "head"), None, None),
            P(("ctx", "head"), None, None),
            P(("ctx", "head"), None, None),
            P(("ctx", "head"), None, None),
        ),
        check_vma=False,
    )
```

profile of v0, /device:TPU:10, one launch (start us, length us, event | category | flops | bytes accessed | tf_op | source)
XLA Modules:
  0.0 160.8 jit_solution(1103698851266385415)
XLA Ops:
  1.9 10.8 %all_to_all.144 = bf16[128,16,128]{2,0,1:T(8,128)(2,1)S(1)} all-to-all(bf16[128,16,128]{2,0,1:T(8,128)(2,1)S(1)} %copy.47), channel_id=1, replica_groups=mesh['ctx'=16,'head'=2] {'head'}, dimensions={1} | all-to-all | bytes 1048576 | tf_op jit(solution)/shard_map/all_to_all | solution.py:63
  12.7 1.9 %collective-permute-start.3 = (bf16[256,8,128]{2,0,1:T(8,128)(2,1)S(1)}, bf16[256,8,128]{2,0,1:T(8,128)(2,1)}, u32[]{:S(2)}, u32[]{:S(2)}) collective-permute-start(bf16[256,8,128]{2,0,1:T(8,128)(2,1)S(1)} %bitcast.94), channel_id=1, source_target_pairs={{0,2},{2,4},{4,6},{6,8},{8,10},{10,12},{12,14},{14,16},{16,18},{18... | collective-permute-start | bytes 1572872 | tf_op jit(solution)/shard_map/ppermute | solution.py:13
  15.9 11.2 %all_to_all.145 = bf16[128,16,128]{2,0,1:T(8,128)(2,1)S(1)} all-to-all(bf16[128,16,128]{2,0,1:T(8,128)(2,1)S(1)} %copy.45), channel_id=1, replica_groups=mesh['ctx'=16,'head'=2] {'head'}, dimensions={1} | all-to-all | bytes 1048576 | tf_op jit(solution)/shard_map/all_to_all | solution.py:64
  27.8 2.4 %collective-permute-start = (bf16[256,8,128]{0,2,1:T(8,128)(2,1)S(1)}, bf16[256,8,128]{0,2,1:T(8,128)(2,1)}, u32[]{:S(2)}, u32[]{:S(2)}) collective-permute-start(bf16[256,8,128]{0,2,1:T(8,128)(2,1)S(1)} %all_to_all.107), channel_id=1, source_target_pairs={{0,2},{2,4},{4,6},{6,8},{8,10},{10,12},{12,14},{14,16},{16,18},{18... | collective-permute-start | bytes 1572872 | tf_op jit(solution)/shard_map/ppermute | solution.py:13
  30.2 3.2 %collective-permute-start.4 = (bf16[256,8,128]{2,0,1:T(8,128)(2,1)}, bf16[256,8,128]{2,0,1:T(8,128)(2,1)}, u32[]{:S(2)}, u32[]{:S(2)}) collective-permute-start(bf16[256,8,128]{2,0,1:T(8,128)(2,1)} %collective-permute-done.3), channel_id=1, source_target_pairs={{0,2},{2,4},{4,6},{6,8},{8,10},{10,12},{12,14},{14,16},{16,18},{18... | collective-permute-start | bytes 1572872 | tf_op jit(solution)/shard_map/ppermute | solution.py:13
  34.3 3.5 %all-to-all-start.2 = ((bf16[128,16,128]{2,0,1:T(8,128)(2,1)}), bf16[128,16,128]{2,0,1:T(8,128)(2,1)S(1)}, u32[]{:S(2)}, u32[]{:S(2)}) async-start(bf16[128,16,128]{2,0,1:T(8,128)(2,1)} %copy.49), calls=%async_computation.2 | async-start | bytes 1048576 | tf_op jit(solution)/shard_map/all_to_all | solution.py:62
  38.9 2.3 %collective-permute-start.1 = (bf16[256,8,128]{0,2,1:T(8,128)(2,1)}, bf16[256,8,128]{0,2,1:T(8,128)(2,1)}, u32[]{:S(2)}, u32[]{:S(2)}) collective-permute-start(bf16[256,8,128]{0,2,1:T(8,128)(2,1)} %collective-permute-done), channel_id=1, source_target_pairs={{0,2},{2,4},{4,6},{6,8},{8,10},{10,12},{12,14},{14,16},{16,18},{18... | collective-permute-start | bytes 1572872 | tf_op jit(solution)/shard_map/ppermute | solution.py:13
  41.2 5.3 %all-to-all-done.2 = bf16[128,16,128]{2,0,1:T(8,128)(2,1)S(1)} async-done(((bf16[128,16,128]{2,0,1:T(8,128)(2,1)}), bf16[128,16,128]{2,0,1:T(8,128)(2,1)S(1)}, u32[]{:S(2)}, u32[]{:S(2)}) %all-to-all-start.2) | async-done | bytes 524320 | tf_op jit(solution)/shard_map/all_to_all | solution.py:62
  46.6 3.5 %all-to-all-start.4 = ((bf16[128,16,128]{2,0,1:T(8,128)(2,1)}), bf16[128,16,128]{2,0,1:T(8,128)(2,1)S(1)}, u32[]{:S(2)}, u32[]{:S(2)}) async-start(bf16[128,16,128]{2,0,1:T(8,128)(2,1)} %copy.54), calls=%async_computation.4 | async-start | bytes 1048576 | tf_op jit(solution)/shard_map/all_to_all | solution.py:65
  50.1 1.9 %collective-permute-start.5 = (bf16[256,8,128]{2,0,1:T(8,128)(2,1)}, bf16[256,8,128]{2,0,1:T(8,128)(2,1)}, u32[]{:S(2)}, u32[]{:S(2)}) collective-permute-start(bf16[256,8,128]{2,0,1:T(8,128)(2,1)} %collective-permute-done.4), channel_id=1, source_target_pairs={{0,2},{2,4},{4,6},{6,8},{8,10},{10,12},{12,14},{14,16},{16,18},{18... | collective-permute-start | bytes 1572872 | tf_op jit(solution)/shard_map/ppermute | solution.py:13
  53.4 4.7 %all-to-all-done.4 = bf16[128,16,128]{2,0,1:T(8,128)(2,1)S(1)} async-done(((bf16[128,16,128]{2,0,1:T(8,128)(2,1)}), bf16[128,16,128]{2,0,1:T(8,128)(2,1)S(1)}, u32[]{:S(2)}, u32[]{:S(2)}) %all-to-all-start.4) | async-done | bytes 524320 | tf_op jit(solution)/shard_map/all_to_all | solution.py:65
  60.1 1.9 %collective-permute-start.2 = (bf16[256,8,128]{0,2,1:T(8,128)(2,1)}, bf16[256,8,128]{0,2,1:T(8,128)(2,1)S(1)}, u32[]{:S(2)}, u32[]{:S(2)}) collective-permute-start(bf16[256,8,128]{0,2,1:T(8,128)(2,1)} %collective-permute-done.1), channel_id=1, source_target_pairs={{0,2},{2,4},{4,6},{6,8},{8,10},{10,12},{12,14},{14,16},{16,18},{18... | collective-permute-start | bytes 1572872 | tf_op jit(solution)/shard_map/ppermute | solution.py:13
  63.1 7.6 %fusion.23 = (f32[8,256]{1,0:T(8,128)S(1)}, f32[8,256,1024]{1,2,0:T(8,128)}) fusion(pred[256,1024]{0,1:T(8,128)(4,1)S(1)} %fusion.16, bf16[256,8,128]{2,0,1:T(8,128)(2,1)} %bitcast.92, bf16[256,8,128]{2,0,1:T(8,128)(2,1)} %collective-permute-done.5, bf16[256,8,128]{2,0,1:T(8,128)(2,1)} %collective-permute-done.4, ...), kind=kOutput, calls=%fused_computation.48 | convolution fusion | flops 553649152 | bytes 11280384 | tf_op jit(solution)/shard_map/sub | solution.py:24
  70.7 4.3 %fusion.6 = bf16[8,256,1024]{1,2,0:T(8,128)(2,1)S(1)} fusion(f32[8,256,1024]{1,2,0:T(8,128)} %get-tuple-element.11, f32[8,256]{1,0:T(8,128)S(1)} %get-tuple-element.10), kind=kLoop, calls=%fused_computation.11 | loop fusion | flops 4194304 | bytes 12591104 | tf_op jit(solution)/shard_map/convert_element_type | solution.py:26
  78.3 3.2 %fusion.24 = (bf16[1024,8,128]{2,0,1:T(8,128)(2,1)S(1)}, f32[1024,8,128]{2,0,1:T(8,128)}) fusion(bf16[8,256,1024]{1,2,0:T(8,128)(2,1)S(1)} %fusion.1, bf16[256,8,128]{2,0,1:T(8,128)(2,1)S(1)} %bitcast.93), kind=kOutput, calls=%fused_computation.49 | convolution fusion | flops 538968064 | bytes 11010048 | tf_op jit(solution)/shard_map/hts,thd->shd/dot_general | solution.py:42
  82.7 3.6 %collective-permute-start.6 = (bf16[256,8,128]{2,0,1:T(8,128)(2,1)}, bf16[256,8,128]{2,0,1:T(8,128)(2,1)}, u32[]{:S(2)}, u32[]{:S(2)}) collective-permute-start(bf16[256,8,128]{2,0,1:T(8,128)(2,1)} %get-tuple-element.7), channel_id=1, source_target_pairs={{2,0},{4,2},{6,4},{8,6},{10,8},{12,10},{14,12},{16,14},{18,16},{20... | collective-permute-start | bytes 1572872 | tf_op jit(solution)/shard_map/ppermute | solution.py:13
  86.4 1.9 %collective-permute-start.8 = (bf16[256,8,128]{2,0,1:T(8,128)(2,1)}, bf16[256,8,128]{2,0,1:T(8,128)(2,1)}, u32[]{:S(2)}, u32[]{:S(2)}) collective-permute-start(bf16[256,8,128]{2,0,1:T(8,128)(2,1)} %get-tuple-element.8), channel_id=1, source_target_pairs={{6,0},{8,2},{10,4},{12,6},{14,8},{16,10},{18,12},{20,14},{22,16},{... | collective-permute-start | bytes 1572872 | tf_op jit(solution)/shard_map/ppermute | solution.py:13
  88.3 3.6 %collective-permute-start.7 = (bf16[256,8,128]{2,0,1:T(8,128)(2,1)}, bf16[256,8,128]{2,0,1:T(8,128)(2,1)}, u32[]{:S(2)}, u32[]{:S(2)}) collective-permute-start(bf16[256,8,128]{2,0,1:T(8,128)(2,1)} %get-tuple-element.9), channel_id=1, source_target_pairs={{4,0},{6,2},{8,4},{10,6},{12,8},{14,10},{16,12},{18,14},{20,16},{2... | collective-permute-start | bytes 1572872 | tf_op jit(solution)/shard_map/ppermute | solution.py:13
  91.9 3.1 %fusion.9 = bf16[256,8,128]{0,2,1:T(8,128)(2,1)} fusion(bf16[8,256,1024]{1,2,0:T(8,128)(2,1)S(1)} %fusion.1, bf16[256,8,128]{2,0,1:T(8,128)(2,1)} %collective-permute-done.5, bf16[256,8,128]{2,0,1:T(8,128)(2,1)} %collective-permute-done.4, bf16[256,8,128]{2,0,1:T(8,128)(2,1)} %collective-permute-done.3, bf16[256,8,128]{2,0,1:T(8,128)(2,1)S(1)} %bitcast.96), kind=kOutput, calls=%fused_computation.18 | convolution fusion | flops 545783808 | bytes 6815744 | tf_op jit(solution)/shard_map/hts,shd->thd/dot_general | solution.py:38
  95.0 3.3 %fusion.25 = (bf16[1024,8,128]{2,0,1:T(8,128)(2,1)S(1)}, f32[1024,8,128]{2,0,1:T(8,128)}) fusion(bf16[8,256,1024]{1,2,0:T(8,128)(2,1)S(1)} %fusion.6, bf16[256,8,128]{0,2,1:T(8,128)(2,1)S(1)} %all_to_all.123), kind=kOutput, calls=%fused_computation.50 | convolution fusion | flops 537919488 | bytes 11010048 | tf_op jit(solution)/shard_map/hts,thd->shd/dot_general | solution.py:45
  98.3 2.1 %copy.60 = bf16[256,8,128]{2,1,0:T(8,128)(2,1)} copy(bf16[256,8,128]{0,2,1:T(8,128)(2,1)} %fusion.9) | data formatting | bytes 1048576 | tf_op jit(solution)/shard_map/convert_element_type | solution.py:40
  100.4 3.5 %all-to-all-start.5 = ((bf16[256,8,128]{2,1,0:T(8,128)(2,1)}), bf16[256,8,128]{2,1,0:T(8,128)(2,1)S(1)}, u32[]{:S(2)}, u32[]{:S(2)}) async-start(bf16[256,8,128]{2,1,0:T(8,128)(2,1)} %copy.60), calls=%async_computation.5 | async-start | bytes 1048576 | tf_op jit(solution)/shard_map/all_to_all | solution.py:106
  105.1 2.0 %collective-permute-start.9 = (bf16[256,8,128]{2,0,1:T(8,128)(2,1)}, bf16[256,8,128]{2,0,1:T(8,128)(2,1)S(1)}, u32[]{:S(2)}, u32[]{:S(2)}) collective-permute-start(bf16[256,8,128]{2,0,1:T(8,128)(2,1)} %get-tuple-element.4), channel_id=1, source_target_pairs={{2,0},{4,2},{6,4},{8,6},{10,8},{12,10},{14,12},{16,14},{18,16},{20... | collective-permute-start | bytes 1572872 | tf_op jit(solution)/shard_map/ppermute | solution.py:13
  107.1 1.9 %collective-permute-start.11 = (bf16[256,8,128]{2,0,1:T(8,128)(2,1)}, bf16[256,8,128]{2,0,1:T(8,128)(2,1)S(1)}, u32[]{:S(2)}, u32[]{:S(2)}) collective-permute-start(bf16[256,8,128]{2,0,1:T(8,128)(2,1)} %get-tuple-element.5), channel_id=1, source_target_pairs={{6,0},{8,2},{10,4},{12,6},{14,8},{16,10},{18,12},{20,14},{22,16},{... | collective-permute-start | bytes 1572872 | tf_op jit(solution)/shard_map/ppermute | solution.py:13
  109.1 1.9 %collective-permute-start.10 = (bf16[256,8,128]{2,0,1:T(8,128)(2,1)}, bf16[256,8,128]{2,0,1:T(8,128)(2,1)}, u32[]{:S(2)}, u32[]{:S(2)}) collective-permute-start(bf16[256,8,128]{2,0,1:T(8,128)(2,1)} %get-tuple-element.6), channel_id=1, source_target_pairs={{4,0},{6,2},{8,4},{10,6},{12,8},{14,10},{16,12},{18,14},{20,16},{2... | collective-permute-start | bytes 1572872 | tf_op jit(solution)/shard_map/ppermute | solution.py:13
  112.6 3.5 %all-to-all-start.3 = ((bf16[256,8,128]{2,1,0:T(8,128)(2,1)}), bf16[256,8,128]{2,1,0:T(8,128)(2,1)S(1)}, u32[]{:S(2)}, u32[]{:S(2)}) async-start(bf16[256,8,128]{2,1,0:T(8,128)(2,1)} %copy.52), calls=%async_computation.3 | async-start | bytes 1048576 | tf_op jit(solution)/shard_map/all_to_all | solution.py:105
  116.1 6.5 %collective-permute-done.7 = bf16[256,8,128]{2,0,1:T(8,128)(2,1)} collective-permute-done((bf16[256,8,128]{2,0,1:T(8,128)(2,1)}, bf16[256,8,128]{2,0,1:T(8,128)(2,1)}, u32[]{:S(2)}, u32[]{:S(2)}) %collective-permute-start.7) | collective-permute-done | bytes 524320 | tf_op jit(solution)/shard_map/ppermute | solution.py:13
  122.6 1.9 %fusion.15 = bf16[256,8,128]{2,0,1:T(8,128)(2,1)S(1)} fusion(f32[1024,8,128]{2,0,1:T(8,128)} %get-tuple-element.15, bf16[256,8,128]{2,0,1:T(8,128)(2,1)} %collective-permute-done.8, bf16[256,8,128]{2,0,1:T(8,128)(2,1)} %collective-permute-done.7, bf16[256,8,128]{2,0,1:T(8,128)(2,1)} %collective-permute-done.6), kind=kLoop, calls=%fused_computation.26 | loop fusion | flops 1835008 | bytes 3145728 | tf_op jit(solution)/shard_map/convert_element_type | solution.py:108
  125.7 3.5 %all-to-all-start.6 = ((bf16[256,8,128]{2,1,0:T(8,128)(2,1)}), bf16[256,8,128]{2,1,0:T(8,128)(2,1)S(1)}, u32[]{:S(2)}, u32[]{:S(2)}) async-start(bf16[256,8,128]{2,1,0:T(8,128)(2,1)} %copy.62), calls=%async_computation.6 | async-start | bytes 1048576 | tf_op jit(solution)/shard_map/all_to_all | solution.py:107
  129.2 17.7 %collective-permute-done.10 = bf16[256,8,128]{2,0,1:T(8,128)(2,1)} collective-permute-done((bf16[256,8,128]{2,0,1:T(8,128)(2,1)}, bf16[256,8,128]{2,0,1:T(8,128)(2,1)}, u32[]{:S(2)}, u32[]{:S(2)}) %collective-permute-start.10) | collective-permute-done | bytes 524320 | tf_op jit(solution)/shard_map/ppermute | solution.py:13
  149.8 3.5 %all-to-all-start.7 = ((bf16[256,8,128]{2,1,0:T(8,128)(2,1)}), bf16[256,8,128]{2,1,0:T(8,128)(2,1)S(1)}, u32[]{:S(2)}, u32[]{:S(2)}) async-start(bf16[256,8,128]{2,1,0:T(8,128)(2,1)} %copy.65), calls=%async_computation.7 | async-start | bytes 1048576 | tf_op jit(solution)/shard_map/all_to_all | solution.py:110
  156.0 3.9 %all-to-all-done.7 = bf16[256,8,128]{2,1,0:T(8,128)(2,1)S(1)} async-done(((bf16[256,8,128]{2,1,0:T(8,128)(2,1)}), bf16[256,8,128]{2,1,0:T(8,128)(2,1)S(1)}, u32[]{:S(2)}, u32[]{:S(2)}) %all-to-all-start.7) | async-done | bytes 524320 | tf_op jit(solution)/shard_map/all_to_all | solution.py:110
  (68 shorter events, 24.4 us)
Async XLA Ops:
  0.6 32.7 %copy-start.1 = (bf16[128,16,128]{2,1,0:T(8,128)(2,1)S(1)}, bf16[128,16,128]{2,1,0:T(8,128)(2,1)}, u32[]{:S(2)}) copy-start(bf16[128,16,128]{2,1,0:T(8,128)(2,1)} %param.5) | copy-start | bytes 1572868
  1.9 35.9 %copy-start.2 = (bf16[128,16,128]{2,1,0:T(8,128)(2,1)S(1)}, bf16[128,16,128]{2,1,0:T(8,128)(2,1)}, u32[]{:S(2)}) copy-start(bf16[128,16,128]{2,1,0:T(8,128)(2,1)} %param.8) | copy-start | bytes 1572868
  12.7 26.1 %copy-start.6 = (s32[1,3]{1,0:T(1,128)S(1)}, s32[1,3]{1,0:T(1,128)}, u32[]{:S(2)}) copy-start(s32[1,3]{1,0:T(1,128)} %param.9) | copy-start | bytes 40
  12.7 33.9 %copy-start.3 = (bf16[128,2,8,128]{3,0,1,2:T(8,128)(2,1)}, bf16[128,2,8,128]{3,0,1,2:T(8,128)(2,1)S(1)}, u32[]{:S(2)}) copy-start(bf16[128,2,8,128]{3,0,1,2:T(8,128)(2,1)S(1)} %copy.48) | copy-start | bytes 1572868
  12.7 17.4 %collective-permute-start.3 = (bf16[256,8,128]{2,0,1:T(8,128)(2,1)S(1)}, bf16[256,8,128]{2,0,1:T(8,128)(2,1)}, u32[]{:S(2)}, u32[]{:S(2)}) collective-permute-start(bf16[256,8,128]{2,0,1:T(8,128)(2,1)S(1)} %bitcast.94), channel_id=1, source_target_pairs={{0,2},{2,4},{4,6},{6,8},{8,10},{10,12},{12,14},{14,16},{16,18},{18... | collective-permute-start | bytes 1572872 | tf_op jit(solution)/shard_map/ppermute | solution.py:13
  27.8 11.2 %collective-permute-start = (bf16[256,8,128]{0,2,1:T(8,128)(2,1)S(1)}, bf16[256,8,128]{0,2,1:T(8,128)(2,1)}, u32[]{:S(2)}, u32[]{:S(2)}) collective-permute-start(bf16[256,8,128]{0,2,1:T(8,128)(2,1)S(1)} %all_to_all.107), channel_id=1, source_target_pairs={{0,2},{2,4},{4,6},{6,8},{8,10},{10,12},{12,14},{14,16},{16,18},{18... | collective-permute-start | bytes 1572872 | tf_op jit(solution)/shard_map/ppermute | solution.py:13
  30.2 19.9 %collective-permute-start.4 = (bf16[256,8,128]{2,0,1:T(8,128)(2,1)}, bf16[256,8,128]{2,0,1:T(8,128)(2,1)}, u32[]{:S(2)}, u32[]{:S(2)}) collective-permute-start(bf16[256,8,128]{2,0,1:T(8,128)(2,1)} %collective-permute-done.3), channel_id=1, source_target_pairs={{0,2},{2,4},{4,6},{6,8},{8,10},{10,12},{12,14},{14,16},{16,18},{18... | collective-permute-start | bytes 1572872 | tf_op jit(solution)/shard_map/ppermute | solution.py:13
  34.3 12.3 %all-to-all-start.2 = ((bf16[128,16,128]{2,0,1:T(8,128)(2,1)}), bf16[128,16,128]{2,0,1:T(8,128)(2,1)S(1)}, u32[]{:S(2)}, u32[]{:S(2)}) async-start(bf16[128,16,128]{2,0,1:T(8,128)(2,1)} %copy.49), calls=%async_computation.2 | async-start | bytes 1048576 | tf_op jit(solution)/shard_map/all_to_all | solution.py:62
  38.9 21.2 %collective-permute-start.1 = (bf16[256,8,128]{0,2,1:T(8,128)(2,1)}, bf16[256,8,128]{0,2,1:T(8,128)(2,1)}, u32[]{:S(2)}, u32[]{:S(2)}) collective-permute-start(bf16[256,8,128]{0,2,1:T(8,128)(2,1)} %collective-permute-done), channel_id=1, source_target_pairs={{0,2},{2,4},{4,6},{6,8},{8,10},{10,12},{12,14},{14,16},{16,18},{18... | collective-permute-start | bytes 1572872 | tf_op jit(solution)/shard_map/ppermute | solution.py:13
  46.6 11.6 %all-to-all-start.4 = ((bf16[128,16,128]{2,0,1:T(8,128)(2,1)}), bf16[128,16,128]{2,0,1:T(8,128)(2,1)S(1)}, u32[]{:S(2)}, u32[]{:S(2)}) async-start(bf16[128,16,128]{2,0,1:T(8,128)(2,1)} %copy.54), calls=%async_computation.4 | async-start | bytes 1048576 | tf_op jit(solution)/shard_map/all_to_all | solution.py:65
  50.1 13.0 %collective-permute-start.5 = (bf16[256,8,128]{2,0,1:T(8,128)(2,1)}, bf16[256,8,128]{2,0,1:T(8,128)(2,1)}, u32[]{:S(2)}, u32[]{:S(2)}) collective-permute-start(bf16[256,8,128]{2,0,1:T(8,128)(2,1)} %collective-permute-done.4), channel_id=1, source_target_pairs={{0,2},{2,4},{4,6},{6,8},{8,10},{10,12},{12,14},{14,16},{16,18},{18... | collective-permute-start | bytes 1572872 | tf_op jit(solution)/shard_map/ppermute | solution.py:13
  60.1 14.9 %collective-permute-start.2 = (bf16[256,8,128]{0,2,1:T(8,128)(2,1)}, bf16[256,8,128]{0,2,1:T(8,128)(2,1)S(1)}, u32[]{:S(2)}, u32[]{:S(2)}) collective-permute-start(bf16[256,8,128]{0,2,1:T(8,128)(2,1)} %collective-permute-done.1), channel_id=1, source_target_pairs={{0,2},{2,4},{4,6},{6,8},{8,10},{10,12},{12,14},{14,16},{16,18},{18... | collective-permute-start | bytes 1572872 | tf_op jit(solution)/shard_map/ppermute | solution.py:13
  70.7 5.2 %slice-start = ((s8[8388608]{0:T(1024)(128)(4,1)}), s8[4194304]{0:T(1024)(128)(4,1)S(1)}, s32[]{:S(2)}) async-start(s8[8388608]{0:T(1024)(128)(4,1)} %bitcast.80), calls=%async_computation.8 | async-start | bytes 8388608
  70.7 5.9 %slice-start.1 = ((s8[8388608]{0:T(1024)(128)(4,1)}), s8[4194304]{0:T(1024)(128)(4,1)S(1)}, s32[]{:S(2)}) async-start(s8[8388608]{0:T(1024)(128)(4,1)} %bitcast.80), calls=%async_computation.9 | async-start | bytes 8388608
  76.6 1.7 %copy-start = (bf16[128,2,8,128]{3,0,1,2:T(8,128)(2,1)S(1)}, bf16[128,2,8,128]{3,0,1,2:T(8,128)(2,1)}, u32[]{:S(2)}) copy-start(bf16[128,2,8,128]{3,0,1,2:T(8,128)(2,1)} %copy.50) | copy-start | bytes 1572868
  78.3 13.6 %copy-start.4 = (bf16[128,2,8,128]{3,0,1,2:T(8,128)(2,1)S(1)}, bf16[128,2,8,128]{3,0,1,2:T(8,128)(2,1)}, u32[]{:S(2)}) copy-start(bf16[128,2,8,128]{3,0,1,2:T(8,128)(2,1)} %copy-done.3) | copy-start | bytes 1572868
  82.7 26.3 %collective-permute-start.6 = (bf16[256,8,128]{2,0,1:T(8,128)(2,1)}, bf16[256,8,128]{2,0,1:T(8,128)(2,1)}, u32[]{:S(2)}, u32[]{:S(2)}) collective-permute-start(bf16[256,8,128]{2,0,1:T(8,128)(2,1)} %get-tuple-element.7), channel_id=1, source_target_pairs={{2,0},{4,2},{6,4},{8,6},{10,8},{12,10},{14,12},{16,14},{18,16},{20... | collective-permute-start | bytes 1572872 | tf_op jit(solution)/shard_map/ppermute | solution.py:13
  86.4 29.7 %collective-permute-start.8 = (bf16[256,8,128]{2,0,1:T(8,128)(2,1)}, bf16[256,8,128]{2,0,1:T(8,128)(2,1)}, u32[]{:S(2)}, u32[]{:S(2)}) collective-permute-start(bf16[256,8,128]{2,0,1:T(8,128)(2,1)} %get-tuple-element.8), channel_id=1, source_target_pairs={{6,0},{8,2},{10,4},{12,6},{14,8},{16,10},{18,12},{20,14},{22,16},{... | collective-permute-start | bytes 1572872 | tf_op jit(solution)/shard_map/ppermute | solution.py:13
  88.3 34.2 %collective-permute-start.7 = (bf16[256,8,128]{2,0,1:T(8,128)(2,1)}, bf16[256,8,128]{2,0,1:T(8,128)(2,1)}, u32[]{:S(2)}, u32[]{:S(2)}) collective-permute-start(bf16[256,8,128]{2,0,1:T(8,128)(2,1)} %get-tuple-element.9), channel_id=1, source_target_pairs={{4,0},{6,2},{8,4},{10,6},{12,8},{14,10},{16,12},{18,14},{20,16},{2... | collective-permute-start | bytes 1572872 | tf_op jit(solution)/shard_map/ppermute | solution.py:13
  100.4 12.2 %all-to-all-start.5 = ((bf16[256,8,128]{2,1,0:T(8,128)(2,1)}), bf16[256,8,128]{2,1,0:T(8,128)(2,1)S(1)}, u32[]{:S(2)}, u32[]{:S(2)}) async-start(bf16[256,8,128]{2,1,0:T(8,128)(2,1)} %copy.60), calls=%async_computation.5 | async-start | bytes 1048576 | tf_op jit(solution)/shard_map/all_to_all | solution.py:106
  105.1 24.1 %collective-permute-start.9 = (bf16[256,8,128]{2,0,1:T(8,128)(2,1)}, bf16[256,8,128]{2,0,1:T(8,128)(2,1)S(1)}, u32[]{:S(2)}, u32[]{:S(2)}) collective-permute-start(bf16[256,8,128]{2,0,1:T(8,128)(2,1)} %get-tuple-element.4), channel_id=1, source_target_pairs={{2,0},{4,2},{6,4},{8,6},{10,8},{12,10},{14,12},{16,14},{18,16},{20... | collective-permute-start | bytes 1572872 | tf_op jit(solution)/shard_map/ppermute | solution.py:13
  107.1 22.0 %collective-permute-start.11 = (bf16[256,8,128]{2,0,1:T(8,128)(2,1)}, bf16[256,8,128]{2,0,1:T(8,128)(2,1)S(1)}, u32[]{:S(2)}, u32[]{:S(2)}) collective-permute-start(bf16[256,8,128]{2,0,1:T(8,128)(2,1)} %get-tuple-element.5), channel_id=1, source_target_pairs={{6,0},{8,2},{10,4},{12,6},{14,8},{16,10},{18,12},{20,14},{22,16},{... | collective-permute-start | bytes 1572872 | tf_op jit(solution)/shard_map/ppermute | solution.py:13
  109.1 37.8 %collective-permute-start.10 = (bf16[256,8,128]{2,0,1:T(8,128)(2,1)}, bf16[256,8,128]{2,0,1:T(8,128)(2,1)}, u32[]{:S(2)}, u32[]{:S(2)}) collective-permute-start(bf16[256,8,128]{2,0,1:T(8,128)(2,1)} %get-tuple-element.6), channel_id=1, source_target_pairs={{4,0},{6,2},{8,4},{10,6},{12,8},{14,10},{16,12},{18,14},{20,16},{2... | collective-permute-start | bytes 1572872 | tf_op jit(solution)/shard_map/ppermute | solution.py:13
  112.6 13.1 %all-to-all-start.3 = ((bf16[256,8,128]{2,1,0:T(8,128)(2,1)}), bf16[256,8,128]{2,1,0:T(8,128)(2,1)S(1)}, u32[]{:S(2)}, u32[]{:S(2)}) async-start(bf16[256,8,128]{2,1,0:T(8,128)(2,1)} %copy.52), calls=%async_computation.3 | async-start | bytes 1048576 | tf_op jit(solution)/shard_map/all_to_all | solution.py:105
  125.7 24.2 %all-to-all-start.6 = ((bf16[256,8,128]{2,1,0:T(8,128)(2,1)}), bf16[256,8,128]{2,1,0:T(8,128)(2,1)S(1)}, u32[]{:S(2)}, u32[]{:S(2)}) async-start(bf16[256,8,128]{2,1,0:T(8,128)(2,1)} %copy.62), calls=%async_computation.6 | async-start | bytes 1048576 | tf_op jit(solution)/shard_map/all_to_all | solution.py:107
  129.2 17.7 %copy-start.5 = (bf16[256,8,128]{2,0,1:T(8,128)(2,1)}, bf16[256,8,128]{2,0,1:T(8,128)(2,1)S(1)}, u32[]{:S(2)}) copy-start(bf16[256,8,128]{2,0,1:T(8,128)(2,1)S(1)} %collective-permute-done.11) | copy-start | bytes 1572868
  149.8 10.1 %all-to-all-start.7 = ((bf16[256,8,128]{2,1,0:T(8,128)(2,1)}), bf16[256,8,128]{2,1,0:T(8,128)(2,1)S(1)}, u32[]{:S(2)}, u32[]{:S(2)}) async-start(bf16[256,8,128]{2,1,0:T(8,128)(2,1)} %copy.65), calls=%async_computation.7 | async-start | bytes 1048576 | tf_op jit(solution)/shard_map/all_to_all | solution.py:110
where the time goes:
time: 162 us; the launch traced here: 161 us
  starting transfers between devices  49.6 us (31%)
  waiting for transfers between devices  38.7 us (24%)
  blocking collectives  22 us (14%)
  local copies, waits for them, and re-layouts  21.2 us (13%)
  matrix products  19.7 us (12%)
  other arithmetic  8.54 us (5%)
    ppermute x12, starting transfers between devices, from_behind(): return lax.ppermute(block, axis, route)  28.6 us
    ppermute x12, waiting for transfers between devices, from_behind(): return lax.ppermute(block, axis, route)  24.2 us
    all_to_all x1, blocking collectives, local(): lax.all_to_all(values, 'head', split_axis=1, concat_axis=0, tiled=True)  11.2 us
    all_to_all x1, blocking collectives, local(): lax.all_to_all(keys, 'head', split_axis=1, concat_axis=0, tiled=True)  10.8 us
    sub x1, matrix products, attend(): weights = jnp.exp(scores - highest)  7.57 us
    unnamed x25, local copies, waits for them, and re-layouts  7.25 us
    all_to_all x1, waiting for transfers between devices, local(): lax.all_to_all(queries, 'head', split_axis=1, concat_axis=0, tiled=True)  5.35 us
    all_to_all x1, waiting for transfers between devices, local(): lax.all_to_all(out_grad, 'head', split_axis=1, concat_axis=0, tiled=True)  4.71 us
  transfers between devices with their start and end apart: 18, of which 6 were waited for; matrix products, arithmetic and copies ran while one was open for 24% of the time, Pallas kernels for 0%

commit v1 on v0

--- a/solution.py
+++ b/solution.py
@@ -103,7 +103,12 @@
         value_total = value_total + back_value.astype(jnp.float32)
     return (
         lax.all_to_all(attended, "head", split_axis=0, concat_axis=1, tiled=True),
-        lax.all_to_all(grad_query, "head", split_axis=0, concat_axis=1, tiled=True),
+        jnp.concatenate(
+            lax.all_to_all(
+                jnp.stack(jnp.split(grad_query, lax.axis_size("head"), axis=0)), "head", 0, 0
+            ),
+            axis=1,
+        ),
         lax.all_to_all(
             key_total.astype(jnp.bfloat16), "head", split_axis=0, concat_axis=1, tiled=True
         ),

time: 162 us -> 171 us (1.056)
  waiting for transfers between devices: 38.7 us -> 44.6 us
    ppermute x12, waiting for transfers between devices: 24.2 us -> 29.7 us  [from_behind(): return lax.ppermute(block, axis, route)]
    unnamed x25 -> x34, local copies, waits for them, and re-layouts: 7.25 us -> 10.3 us
    convert_element_type x1 -> x0, local copies, waits for them, and re-layouts: 2.12 us -> none  [attend(): grad_query = (jnp.einsum('hts,shd->thd', grad_scores, key_window, preferr...]
    concatenate x1, local copies, waits for them, and re-layouts: 0.06 us -> 1.89 us  [local(): value_window = jnp.concatenate(value_tiles, axis=0)]
  transfers between devices with their start and end apart: 18 -> 18, of which waited for: 6 -> 7; matrix products, arithmetic and copies ran while one was open for 24% -> 22% of each run, Pallas kernels for 0% -> 0%
where the time goes in v1:
time: 171 us; the launch traced here: 170 us
  starting transfers between devices  49.6 us (29%)
  waiting for transfers between devices  44.6 us (26%)
  local copies, waits for them, and re-layouts  22.4 us (13%)
  blocking collectives  22 us (13%)
  matrix products  21.2 us (12%)
  other arithmetic  9.36 us (5%)
    ppermute x12, waiting for transfers between devices, from_behind(): return lax.ppermute(block, axis, route)  29.7 us
    ppermute x12, starting transfers between devices, from_behind(): return lax.ppermute(block, axis, route)  28.6 us
    all_to_all x1, blocking collectives, local(): lax.all_to_all(values, 'head', split_axis=1, concat_axis=0, tiled=True)  11.2 us
    all_to_all x1, blocking collectives, local(): lax.all_to_all(keys, 'head', split_axis=1, concat_axis=0, tiled=True)  10.8 us
    unnamed x34, local copies, waits for them, and re-layouts  10.3 us
    sub x1, matrix products, attend(): weights = jnp.exp(scores - highest)  7.09 us
    all_to_all x1, waiting for transfers between devices, local(): lax.all_to_all(out_grad, 'head', split_axis=1, concat_axis=0, tiled=True)  5.48 us
    all_to_all x1, waiting for transfers between devices, local(): lax.all_to_all(queries, 'head', split_axis=1, concat_axis=0, tiled=True)  5.35 us
  transfers between devices with their start and end apart: 18, of which 7 were waited for; matrix products, arithmetic and copies ran while one was open for 22% of the time, Pallas kernels for 0%

profile of v1, /device:TPU:10, one launch (start us, length us, event | category | flops | bytes accessed | tf_op | source)
XLA Modules:
  0.0 170.2 jit_solution(16244883051528491758)
XLA Ops:
  1.9 10.8 %all_to_all.131 = bf16[128,16,128]{2,0,1:T(8,128)(2,1)S(1)} all-to-all(bf16[128,16,128]{2,0,1:T(8,128)(2,1)S(1)} %copy.46), channel_id=1, replica_groups=mesh['ctx'=16,'head'=2] {'head'}, dimensions={1} | all-to-all | bytes 1048576 | tf_op jit(solution)/shard_map/all_to_all | solution.py:63
  12.7 1.9 %collective-permute-start.3 = (bf16[256,8,128]{2,0,1:T(8,128)(2,1)S(1)}, bf16[256,8,128]{2,0,1:T(8,128)(2,1)S(1)}, u32[]{:S(2)}, u32[]{:S(2)}) collective-permute-start(bf16[256,8,128]{2,0,1:T(8,128)(2,1)S(1)} %bitcast.95), channel_id=1, source_target_pairs={{0,2},{2,4},{4,6},{6,8},{8,10},{10,12},{12,14},{14,16},{16,18},{18... | collective-permute-start | bytes 1572872 | tf_op jit(solution)/shard_map/ppermute | solution.py:13
  15.9 11.2 %all_to_all.132 = bf16[128,16,128]{2,0,1:T(8,128)(2,1)S(1)} all-to-all(bf16[128,16,128]{2,0,1:T(8,128)(2,1)S(1)} %copy.44), channel_id=1, replica_groups=mesh['ctx'=16,'head'=2] {'head'}, dimensions={1} | all-to-all | bytes 1048576 | tf_op jit(solution)/shard_map/all_to_all | solution.py:64
  27.8 2.4 %collective-permute-start = (bf16[256,8,128]{0,2,1:T(8,128)(2,1)S(1)}, bf16[256,8,128]{0,2,1:T(8,128)(2,1)}, u32[]{:S(2)}, u32[]{:S(2)}) collective-permute-start(bf16[256,8,128]{0,2,1:T(8,128)(2,1)S(1)} %all_to_all.97), channel_id=1, source_target_pairs={{0,2},{2,4},{4,6},{6,8},{8,10},{10,12},{12,14},{14,16},{16,18},{18... | collective-permute-start | bytes 1572872 | tf_op jit(solution)/shard_map/ppermute | solution.py:13
  30.2 3.2 %collective-permute-start.4 = (bf16[256,8,128]{2,0,1:T(8,128)(2,1)S(1)}, bf16[256,8,128]{2,0,1:T(8,128)(2,1)}, u32[]{:S(2)}, u32[]{:S(2)}) collective-permute-start(bf16[256,8,128]{2,0,1:T(8,128)(2,1)S(1)} %collective-permute-done.3), channel_id=1, source_target_pairs={{0,2},{2,4},{4,6},{6,8},{8,10},{10,12},{12,14},{14,16},{16,18},{18... | collective-permute-start | bytes 1572872 | tf_op jit(solution)/shard_map/ppermute | solution.py:13
  34.3 3.5 %all-to-all-start.2 = ((bf16[128,16,128]{2,0,1:T(8,128)(2,1)}), bf16[128,16,128]{2,0,1:T(8,128)(2,1)S(1)}, u32[]{:S(2)}, u32[]{:S(2)}) async-start(bf16[128,16,128]{2,0,1:T(8,128)(2,1)} %copy.48), calls=%async_computation.2 | async-start | bytes 1048576 | tf_op jit(solution)/shard_map/all_to_all | solution.py:62
  38.9 2.3 %collective-permute-start.1 = (bf16[256,8,128]{0,2,1:T(8,128)(2,1)}, bf16[256,8,128]{0,2,1:T(8,128)(2,1)}, u32[]{:S(2)}, u32[]{:S(2)}) collective-permute-start(bf16[256,8,128]{0,2,1:T(8,128)(2,1)} %collective-permute-done), channel_id=1, source_target_pairs={{0,2},{2,4},{4,6},{6,8},{8,10},{10,12},{12,14},{14,16},{16,18},{18... | collective-permute-start | bytes 1572872 | tf_op jit(solution)/shard_map/ppermute | solution.py:13
  41.3 5.3 %all-to-all-done.2 = bf16[128,16,128]{2,0,1:T(8,128)(2,1)S(1)} async-done(((bf16[128,16,128]{2,0,1:T(8,128)(2,1)}), bf16[128,16,128]{2,0,1:T(8,128)(2,1)S(1)}, u32[]{:S(2)}, u32[]{:S(2)}) %all-to-all-start.2) | async-done | bytes 524320 | tf_op jit(solution)/shard_map/all_to_all | solution.py:62
  46.6 3.5 %all-to-all-start.4 = ((bf16[128,16,128]{2,0,1:T(8,128)(2,1)}), bf16[128,16,128]{2,0,1:T(8,128)(2,1)S(1)}, u32[]{:S(2)}, u32[]{:S(2)}) async-start(bf16[128,16,128]{2,0,1:T(8,128)(2,1)} %copy.53), calls=%async_computation.4 | async-start | bytes 1048576 | tf_op jit(solution)/shard_map/all_to_all | solution.py:65
  50.1 1.9 %collective-permute-start.5 = (bf16[256,8,128]{2,0,1:T(8,128)(2,1)}, bf16[256,8,128]{2,0,1:T(8,128)(2,1)}, u32[]{:S(2)}, u32[]{:S(2)}) collective-permute-start(bf16[256,8,128]{2,0,1:T(8,128)(2,1)} %collective-permute-done.4), channel_id=1, source_target_pairs={{0,2},{2,4},{4,6},{6,8},{8,10},{10,12},{12,14},{14,16},{16,18},{18... | collective-permute-start | bytes 1572872 | tf_op jit(solution)/shard_map/ppermute | solution.py:13
  52.7 5.5 %all-to-all-done.4 = bf16[128,16,128]{2,0,1:T(8,128)(2,1)S(1)} async-done(((bf16[128,16,128]{2,0,1:T(8,128)(2,1)}), bf16[128,16,128]{2,0,1:T(8,128)(2,1)S(1)}, u32[]{:S(2)}, u32[]{:S(2)}) %all-to-all-start.4) | async-done | bytes 524320 | tf_op jit(solution)/shard_map/all_to_all | solution.py:65
  63.7 1.9 %constant_dynamic-update-slice_fusion.1 = bf16[1024,8,128]{0,2,1:T(8,128)(2,1)} fusion(bf16[1024,8,128]{0,2,1:T(8,128)(2,1)} %constant_dynamic-update-slice_fusion.2, bf16[256,8,128]{0,2,1:T(8,128)(2,1)} %collective-permute-done.1), kind=kLoop, calls=%fused_computation.39 | loop fusion | bytes 1048576
  65.7 7.1 %fusion.23 = (f32[8,256]{1,0:T(8,128)S(1)}, f32[8,256,1024]{1,2,0:T(8,128)}) fusion(pred[256,1024]{0,1:T(8,128)(4,1)S(1)} %fusion.16, bf16[256,8,128]{2,0,1:T(8,128)(2,1)S(1)} %bitcast.93, bf16[256,8,128]{2,0,1:T(8,128)(2,1)} %collective-permute-done.5, bf16[256,8,128]{2,0,1:T(8,128)(2,1)} %collective-permute-done.4, ...), kind=kOutput, calls=%fused_computation.50 | convolution fusion | flops 553649152 | bytes 11280384 | tf_op jit(solution)/shard_map/sub | solution.py:24
  72.7 4.3 %fusion.6 = bf16[8,256,1024]{1,2,0:T(8,128)(2,1)S(1)} fusion(f32[8,256,1024]{1,2,0:T(8,128)} %get-tuple-element.25, f32[8,256]{1,0:T(8,128)S(1)} %get-tuple-element.24), kind=kLoop, calls=%fused_computation.11 | loop fusion | flops 4194304 | bytes 12591104 | tf_op jit(solution)/shard_map/convert_element_type | solution.py:26
  77.0 3.3 %fusion.25 = (bf16[1024,8,128]{2,0,1:T(8,128)(2,1)S(1)}, f32[1024,8,128]{2,0,1:T(8,128)}) fusion(bf16[8,256,1024]{1,2,0:T(8,128)(2,1)S(1)} %fusion.6, bf16[256,8,128]{0,2,1:T(8,128)(2,1)S(1)} %all_to_all.113), kind=kOutput, calls=%fused_computation.52 | convolution fusion | flops 537919488 | bytes 11010048 | tf_op jit(solution)/shard_map/hts,thd->shd/dot_general | solution.py:45
  82.2 2.3 %multiply_reduce_fusion = (f32[256,8]{0,1:T(8,128)S(1)}, bf16[256,8,128]{0,2,1:T(8,128)(2,1)S(1)}) fusion(bf16[256,8,128]{0,2,1:T(8,128)(2,1)S(1)} %all_to_all.113, bf16[1024,8,128]{0,2,1:T(8,128)(2,1)} %constant_dynamic-update-slice_fusion, bf16[8,256,1024]{1,2,0:T(8,128)(2,1)S(1)} %fusion.6), kind=kOutput, calls=%fused_computation.27 | convolution fusion | flops 538179584 | bytes 7348224 | tf_op jit(solution)/shard_map/hts,shd->thd/dot_general | solution.py:27
  84.6 3.2 %fusion.1 = bf16[8,256,1024]{1,2,0:T(8,128)(2,1)S(1)} fusion(f32[8,256]{1,0:T(8,128)S(1)} %bitcast.101, f32[8,256,1024]{1,2,0:T(8,128)S(1)} %bitcast.82, f32[8,256]{1,0:T(8,128)S(1)} %get-tuple-element.24, bf16[1024,8,128]{0,2,1:T(8,128)(2,1)} %constant_dynamic-update-slice_fusion, bf16[256,8,128]{0,2,1:T(8,128)(2,1)S(1)} %all_to_all.113), kind=kOutput, calls=%fused_computation.2 | convolution fusion | flops 545259520 | bytes 15220736 | tf_op jit(solution)/shard_map/thd,shd->hts/dot_general | solution.py:30
  87.8 3.2 %fusion.24 = (bf16[1024,8,128]{2,0,1:T(8,128)(2,1)S(1)}, f32[1024,8,128]{2,0,1:T(8,128)}) fusion(bf16[8,256,1024]{1,2,0:T(8,128)(2,1)S(1)} %fusion.1, bf16[256,8,128]{2,0,1:T(8,128)(2,1)S(1)} %bitcast.94), kind=kOutput, calls=%fused_computation.51 | convolution fusion | flops 538968064 | bytes 11010048 | tf_op jit(solution)/shard_map/hts,thd->shd/dot_general | solution.py:42
  92.2 3.8 %collective-permute-start.6 = (bf16[256,8,128]{2,0,1:T(8,128)(2,1)}, bf16[256,8,128]{2,0,1:T(8,128)(2,1)}, u32[]{:S(2)}, u32[]{:S(2)}) collective-permute-start(bf16[256,8,128]{2,0,1:T(8,128)(2,1)} %get-tuple-element.19), channel_id=1, source_target_pairs={{2,0},{4,2},{6,4},{8,6},{10,8},{12,10},{14,12},{16,14},{18,16},{20... | collective-permute-start | bytes 1572872 | tf_op jit(solution)/shard_map/ppermute | solution.py:13
  96.0 2.1 %fusion.9 = bf16[256,8,128]{0,2,1:T(8,128)(2,1)S(1)} fusion(bf16[8,256,1024]{1,2,0:T(8,128)(2,1)S(1)} %fusion.1, bf16[256,8,128]{2,0,1:T(8,128)(2,1)} %collective-permute-done.5, bf16[256,8,128]{2,0,1:T(8,128)(2,1)} %collective-permute-done.4, bf16[256,8,128]{2,0,1:T(8,128)(2,1)S(1)} %copy-done.9, bf16[256,8,128]{2,0,1:T(8,128)(2,1)S(1)} %bitcast.97), kind=kOutput, calls=%fused_computation.18 | convolution fusion | flops 545783808 | bytes 6815744 | tf_op jit(solution)/shard_map/hts,shd->thd/dot_general | solution.py:38
  98.3 1.9 %collective-permute-start.8 = (bf16[256,8,128]{2,0,1:T(8,128)(2,1)}, bf16[256,8,128]{2,0,1:T(8,128)(2,1)}, u32[]{:S(2)}, u32[]{:S(2)}) collective-permute-start(bf16[256,8,128]{2,0,1:T(8,128)(2,1)} %get-tuple-element.20), channel_id=1, source_target_pairs={{6,0},{8,2},{10,4},{12,6},{14,8},{16,10},{18,12},{20,14},{22,16},{... | collective-permute-start | bytes 1572872 | tf_op jit(solution)/shard_map/ppermute | solution.py:13
  100.2 3.4 %collective-permute-start.7 = (bf16[256,8,128]{2,0,1:T(8,128)(2,1)}, bf16[256,8,128]{2,0,1:T(8,128)(2,1)}, u32[]{:S(2)}, u32[]{:S(2)}) collective-permute-start(bf16[256,8,128]{2,0,1:T(8,128)(2,1)} %get-tuple-element.21), channel_id=1, source_target_pairs={{4,0},{6,2},{8,4},{10,6},{12,8},{14,10},{16,12},{18,14},{20,16},{2... | collective-permute-start | bytes 1572872 | tf_op jit(solution)/shard_map/ppermute | solution.py:13
  104.4 3.5 %all-to-all-start.5 = ((bf16[2,128,8,128]{1,3,2,0:T(8,128)(2,1)}), bf16[2,128,8,128]{1,3,2,0:T(8,128)(2,1)S(1)}, u32[]{:S(2)}, u32[]{:S(2)}) async-start(bf16[2,128,8,128]{1,3,2,0:T(8,128)(2,1)} %pad_maximum_fusion.1), calls=%async_computation.5 | async-start | bytes 1048576 | tf_op jit(solution)/shard_map/all_to_all | solution.py:107
  109.1 2.0 %collective-permute-start.9 = (bf16[256,8,128]{2,0,1:T(8,128)(2,1)}, bf16[256,8,128]{2,0,1:T(8,128)(2,1)S(1)}, u32[]{:S(2)}, u32[]{:S(2)}) collective-permute-start(bf16[256,8,128]{2,0,1:T(8,128)(2,1)} %get-tuple-element.16), channel_id=1, source_target_pairs={{2,0},{4,2},{6,4},{8,6},{10,8},{12,10},{14,12},{16,14},{18,16},{20... | collective-permute-start | bytes 1572872 | tf_op jit(solution)/shard_map/ppermute | solution.py:13
  111.2 1.9 %collective-permute-start.11 = (bf16[256,8,128]{2,0,1:T(8,128)(2,1)}, bf16[256,8,128]{2,0,1:T(8,128)(2,1)S(1)}, u32[]{:S(2)}, u32[]{:S(2)}) collective-permute-start(bf16[256,8,128]{2,0,1:T(8,128)(2,1)} %get-tuple-element.17), channel_id=1, source_target_pairs={{6,0},{8,2},{10,4},{12,6},{14,8},{16,10},{18,12},{20,14},{22,16},{... | collective-permute-start | bytes 1572872 | tf_op jit(solution)/shard_map/ppermute | solution.py:13
  113.1 1.9 %collective-permute-start.10 = (bf16[256,8,128]{2,0,1:T(8,128)(2,1)}, bf16[256,8,128]{2,0,1:T(8,128)(2,1)}, u32[]{:S(2)}, u32[]{:S(2)}) collective-permute-start(bf16[256,8,128]{2,0,1:T(8,128)(2,1)} %get-tuple-element.18), channel_id=1, source_target_pairs={{4,0},{6,2},{8,4},{10,6},{12,8},{14,10},{16,12},{18,14},{20,16},{2... | collective-permute-start | bytes 1572872 | tf_op jit(solution)/shard_map/ppermute | solution.py:13
  116.6 3.5 %all-to-all-start.3 = ((bf16[256,8,128]{2,1,0:T(8,128)(2,1)}), bf16[256,8,128]{2,1,0:T(8,128)(2,1)S(1)}, u32[]{:S(2)}, u32[]{:S(2)}) async-start(bf16[256,8,128]{2,1,0:T(8,128)(2,1)} %copy.51), calls=%async_computation.3 | async-start | bytes 1048576 | tf_op jit(solution)/shard_map/all_to_all | solution.py:105
  120.1 9.5 %collective-permute-done.7 = bf16[256,8,128]{2,0,1:T(8,128)(2,1)} collective-permute-done((bf16[256,8,128]{2,0,1:T(8,128)(2,1)}, bf16[256,8,128]{2,0,1:T(8,128)(2,1)}, u32[]{:S(2)}, u32[]{:S(2)}) %collective-permute-start.7) | collective-permute-done | bytes 524320 | tf_op jit(solution)/shard_map/ppermute | solution.py:13
  132.6 3.5 %all-to-all-start.6 = ((bf16[256,8,128]{2,1,0:T(8,128)(2,1)}), bf16[256,8,128]{2,1,0:T(8,128)(2,1)S(1)}, u32[]{:S(2)}, u32[]{:S(2)}) async-start(bf16[256,8,128]{2,1,0:T(8,128)(2,1)} %copy.59), calls=%async_computation.6 | async-start | bytes 1048576 | tf_op jit(solution)/shard_map/all_to_all | solution.py:112
  138.0 18.3 %collective-permute-done.10 = bf16[256,8,128]{2,0,1:T(8,128)(2,1)} collective-permute-done((bf16[256,8,128]{2,0,1:T(8,128)(2,1)}, bf16[256,8,128]{2,0,1:T(8,128)(2,1)}, u32[]{:S(2)}, u32[]{:S(2)}) %collective-permute-start.10) | collective-permute-done | bytes 524320 | tf_op jit(solution)/shard_map/ppermute | solution.py:13
  159.2 3.5 %all-to-all-start.7 = ((bf16[256,8,128]{2,1,0:T(8,128)(2,1)}), bf16[256,8,128]{2,1,0:T(8,128)(2,1)S(1)}, u32[]{:S(2)}, u32[]{:S(2)}) async-start(bf16[256,8,128]{2,1,0:T(8,128)(2,1)} %copy.62), calls=%async_computation.7 | async-start | bytes 1048576 | tf_op jit(solution)/shard_map/all_to_all | solution.py:115
  165.7 3.6 %all-to-all-done.7 = bf16[256,8,128]{2,1,0:T(8,128)(2,1)S(1)} async-done(((bf16[256,8,128]{2,1,0:T(8,128)(2,1)}), bf16[256,8,128]{2,1,0:T(8,128)(2,1)S(1)}, u32[]{:S(2)}, u32[]{:S(2)}) %all-to-all-start.7) | async-done | bytes 524320 | tf_op jit(solution)/shard_map/all_to_all | solution.py:115
  (77 shorter events, 29.9 us)
Async XLA Ops:
  0.6 32.7 %copy-start.2 = (bf16[128,16,128]{2,1,0:T(8,128)(2,1)S(1)}, bf16[128,16,128]{2,1,0:T(8,128)(2,1)}, u32[]{:S(2)}) copy-start(bf16[128,16,128]{2,1,0:T(8,128)(2,1)} %param.5) | copy-start | bytes 1572868
  1.9 35.9 %copy-start.3 = (bf16[128,16,128]{2,1,0:T(8,128)(2,1)S(1)}, bf16[128,16,128]{2,1,0:T(8,128)(2,1)}, u32[]{:S(2)}) copy-start(bf16[128,16,128]{2,1,0:T(8,128)(2,1)} %param.8) | copy-start | bytes 1572868
  12.7 26.1 %copy-start.10 = (s32[1,3]{1,0:T(1,128)S(1)}, s32[1,3]{1,0:T(1,128)}, u32[]{:S(2)}) copy-start(s32[1,3]{1,0:T(1,128)} %param.9) | copy-start | bytes 40
  12.7 52.9 %copy-start.4 = (bf16[128,2,8,128]{3,0,1,2:T(8,128)(2,1)}, bf16[128,2,8,128]{3,0,1,2:T(8,128)(2,1)S(1)}, u32[]{:S(2)}) copy-start(bf16[128,2,8,128]{3,0,1,2:T(8,128)(2,1)S(1)} %copy.47) | copy-start | bytes 1572868
  12.7 17.4 %collective-permute-start.3 = (bf16[256,8,128]{2,0,1:T(8,128)(2,1)S(1)}, bf16[256,8,128]{2,0,1:T(8,128)(2,1)S(1)}, u32[]{:S(2)}, u32[]{:S(2)}) collective-permute-start(bf16[256,8,128]{2,0,1:T(8,128)(2,1)S(1)} %bitcast.95), channel_id=1, source_target_pairs={{0,2},{2,4},{4,6},{6,8},{8,10},{10,12},{12,14},{14,16},{16,18},{18... | collective-permute-start | bytes 1572872 | tf_op jit(solution)/shard_map/ppermute | solution.py:13
  27.8 11.2 %collective-permute-start = (bf16[256,8,128]{0,2,1:T(8,128)(2,1)S(1)}, bf16[256,8,128]{0,2,1:T(8,128)(2,1)}, u32[]{:S(2)}, u32[]{:S(2)}) collective-permute-start(bf16[256,8,128]{0,2,1:T(8,128)(2,1)S(1)} %all_to_all.97), channel_id=1, source_target_pairs={{0,2},{2,4},{4,6},{6,8},{8,10},{10,12},{12,14},{14,16},{16,18},{18... | collective-permute-start | bytes 1572872 | tf_op jit(solution)/shard_map/ppermute | solution.py:13
  30.2 28.4 %copy-start.7 = (bf16[256,8,128]{2,0,1:T(8,128)(2,1)}, bf16[256,8,128]{2,0,1:T(8,128)(2,1)S(1)}, u32[]{:S(2)}) copy-start(bf16[256,8,128]{2,0,1:T(8,128)(2,1)S(1)} %collective-permute-done.3) | copy-start | bytes 1572868
  30.2 19.9 %collective-permute-start.4 = (bf16[256,8,128]{2,0,1:T(8,128)(2,1)S(1)}, bf16[256,8,128]{2,0,1:T(8,128)(2,1)}, u32[]{:S(2)}, u32[]{:S(2)}) collective-permute-start(bf16[256,8,128]{2,0,1:T(8,128)(2,1)S(1)} %collective-permute-done.3), channel_id=1, source_target_pairs={{0,2},{2,4},{4,6},{6,8},{8,10},{10,12},{12,14},{14,16},{16,18},{18... | collective-permute-start | bytes 1572872 | tf_op jit(solution)/shard_map/ppermute | solution.py:13
  34.3 12.3 %all-to-all-start.2 = ((bf16[128,16,128]{2,0,1:T(8,128)(2,1)}), bf16[128,16,128]{2,0,1:T(8,128)(2,1)S(1)}, u32[]{:S(2)}, u32[]{:S(2)}) async-start(bf16[128,16,128]{2,0,1:T(8,128)(2,1)} %copy.48), calls=%async_computation.2 | async-start | bytes 1048576 | tf_op jit(solution)/shard_map/all_to_all | solution.py:62
  38.9 22.8 %collective-permute-start.1 = (bf16[256,8,128]{0,2,1:T(8,128)(2,1)}, bf16[256,8,128]{0,2,1:T(8,128)(2,1)}, u32[]{:S(2)}, u32[]{:S(2)}) collective-permute-start(bf16[256,8,128]{0,2,1:T(8,128)(2,1)} %collective-permute-done), channel_id=1, source_target_pairs={{0,2},{2,4},{4,6},{6,8},{8,10},{10,12},{12,14},{14,16},{16,18},{18... | collective-permute-start | bytes 1572872 | tf_op jit(solution)/shard_map/ppermute | solution.py:13
  46.6 11.6 %all-to-all-start.4 = ((bf16[128,16,128]{2,0,1:T(8,128)(2,1)}), bf16[128,16,128]{2,0,1:T(8,128)(2,1)S(1)}, u32[]{:S(2)}, u32[]{:S(2)}) async-start(bf16[128,16,128]{2,0,1:T(8,128)(2,1)} %copy.53), calls=%async_computation.4 | async-start | bytes 1048576 | tf_op jit(solution)/shard_map/all_to_all | solution.py:65
  50.1 15.5 %collective-permute-start.5 = (bf16[256,8,128]{2,0,1:T(8,128)(2,1)}, bf16[256,8,128]{2,0,1:T(8,128)(2,1)}, u32[]{:S(2)}, u32[]{:S(2)}) collective-permute-start(bf16[256,8,128]{2,0,1:T(8,128)(2,1)} %collective-permute-done.4), channel_id=1, source_target_pairs={{0,2},{2,4},{4,6},{6,8},{8,10},{10,12},{12,14},{14,16},{16,18},{18... | collective-permute-start | bytes 1572872 | tf_op jit(solution)/shard_map/ppermute | solution.py:13
  52.7 20.1 %copy-start = (bf16[128,2,8,128]{3,0,1,2:T(8,128)(2,1)}, bf16[128,2,8,128]{3,0,1,2:T(8,128)(2,1)S(1)}, u32[]{:S(2)}) copy-start(bf16[128,2,8,128]{3,0,1,2:T(8,128)(2,1)S(1)} %copy.49) | copy-start | bytes 1572868
  58.6 7.1 %copy-start.8 = (bf16[256,8,128]{2,0,1:T(8,128)(2,1)S(1)}, bf16[256,8,128]{2,0,1:T(8,128)(2,1)}, u32[]{:S(2)}) copy-start(bf16[256,8,128]{2,0,1:T(8,128)(2,1)} %copy-done.7) | copy-start | bytes 1572868
  61.8 18.5 %collective-permute-start.2 = (bf16[256,8,128]{0,2,1:T(8,128)(2,1)}, bf16[256,8,128]{0,2,1:T(8,128)(2,1)}, u32[]{:S(2)}, u32[]{:S(2)}) collective-permute-start(bf16[256,8,128]{0,2,1:T(8,128)(2,1)} %collective-permute-done.1), channel_id=1, source_target_pairs={{0,2},{2,4},{4,6},{6,8},{8,10},{10,12},{12,14},{14,16},{16,18},{18... | collective-permute-start | bytes 1572872 | tf_op jit(solution)/shard_map/ppermute | solution.py:13
  72.7 11.8 %slice-start = ((s8[8388608]{0:T(1024)(128)(4,1)}), s8[4194304]{0:T(1024)(128)(4,1)S(1)}, s32[]{:S(2)}) async-start(s8[8388608]{0:T(1024)(128)(4,1)} %bitcast.81), calls=%async_computation.8 | async-start | bytes 8388608
  77.0 7.5 %slice-start.1 = ((s8[8388608]{0:T(1024)(128)(4,1)}), s8[4194304]{0:T(1024)(128)(4,1)S(1)}, s32[]{:S(2)}) async-start(s8[8388608]{0:T(1024)(128)(4,1)} %bitcast.81), calls=%async_computation.9 | async-start | bytes 8388608
  84.5 3.2 %copy-start.1 = (bf16[128,2,8,128]{3,0,1,2:T(8,128)(2,1)S(1)}, bf16[128,2,8,128]{3,0,1,2:T(8,128)(2,1)}, u32[]{:S(2)}) copy-start(bf16[128,2,8,128]{3,0,1,2:T(8,128)(2,1)} %copy-done) | copy-start | bytes 1572868
  87.8 8.2 %copy-start.5 = (bf16[128,2,8,128]{3,0,1,2:T(8,128)(2,1)S(1)}, bf16[128,2,8,128]{3,0,1,2:T(8,128)(2,1)}, u32[]{:S(2)}) copy-start(bf16[128,2,8,128]{3,0,1,2:T(8,128)(2,1)} %copy-done.4) | copy-start | bytes 1572868
  87.8 8.2 %copy-start.9 = (bf16[256,8,128]{2,0,1:T(8,128)(2,1)S(1)}, bf16[256,8,128]{2,0,1:T(8,128)(2,1)}, u32[]{:S(2)}) copy-start(bf16[256,8,128]{2,0,1:T(8,128)(2,1)} %copy-done.7) | copy-start | bytes 1572868
  92.2 20.9 %collective-permute-start.6 = (bf16[256,8,128]{2,0,1:T(8,128)(2,1)}, bf16[256,8,128]{2,0,1:T(8,128)(2,1)}, u32[]{:S(2)}, u32[]{:S(2)}) collective-permute-start(bf16[256,8,128]{2,0,1:T(8,128)(2,1)} %get-tuple-element.19), channel_id=1, source_target_pairs={{2,0},{4,2},{6,4},{8,6},{10,8},{12,10},{14,12},{16,14},{18,16},{20... | collective-permute-start | bytes 1572872 | tf_op jit(solution)/shard_map/ppermute | solution.py:13
  98.3 21.8 %collective-permute-start.8 = (bf16[256,8,128]{2,0,1:T(8,128)(2,1)}, bf16[256,8,128]{2,0,1:T(8,128)(2,1)}, u32[]{:S(2)}, u32[]{:S(2)}) collective-permute-start(bf16[256,8,128]{2,0,1:T(8,128)(2,1)} %get-tuple-element.20), channel_id=1, source_target_pairs={{6,0},{8,2},{10,4},{12,6},{14,8},{16,10},{18,12},{20,14},{22,16},{... | collective-permute-start | bytes 1572872 | tf_op jit(solution)/shard_map/ppermute | solution.py:13
  100.2 29.4 %collective-permute-start.7 = (bf16[256,8,128]{2,0,1:T(8,128)(2,1)}, bf16[256,8,128]{2,0,1:T(8,128)(2,1)}, u32[]{:S(2)}, u32[]{:S(2)}) collective-permute-start(bf16[256,8,128]{2,0,1:T(8,128)(2,1)} %get-tuple-element.21), channel_id=1, source_target_pairs={{4,0},{6,2},{8,4},{10,6},{12,8},{14,10},{16,12},{18,14},{20,16},{2... | collective-permute-start | bytes 1572872 | tf_op jit(solution)/shard_map/ppermute | solution.py:13
  104.4 12.1 %all-to-all-start.5 = ((bf16[2,128,8,128]{1,3,2,0:T(8,128)(2,1)}), bf16[2,128,8,128]{1,3,2,0:T(8,128)(2,1)S(1)}, u32[]{:S(2)}, u32[]{:S(2)}) async-start(bf16[2,128,8,128]{1,3,2,0:T(8,128)(2,1)} %pad_maximum_fusion.1), calls=%async_computation.5 | async-start | bytes 1048576 | tf_op jit(solution)/shard_map/all_to_all | solution.py:107
  109.1 27.0 %collective-permute-start.9 = (bf16[256,8,128]{2,0,1:T(8,128)(2,1)}, bf16[256,8,128]{2,0,1:T(8,128)(2,1)S(1)}, u32[]{:S(2)}, u32[]{:S(2)}) collective-permute-start(bf16[256,8,128]{2,0,1:T(8,128)(2,1)} %get-tuple-element.16), channel_id=1, source_target_pairs={{2,0},{4,2},{6,4},{8,6},{10,8},{12,10},{14,12},{16,14},{18,16},{20... | collective-permute-start | bytes 1572872 | tf_op jit(solution)/shard_map/ppermute | solution.py:13
  111.2 26.9 %collective-permute-start.11 = (bf16[256,8,128]{2,0,1:T(8,128)(2,1)}, bf16[256,8,128]{2,0,1:T(8,128)(2,1)S(1)}, u32[]{:S(2)}, u32[]{:S(2)}) collective-permute-start(bf16[256,8,128]{2,0,1:T(8,128)(2,1)} %get-tuple-element.17), channel_id=1, source_target_pairs={{6,0},{8,2},{10,4},{12,6},{14,8},{16,10},{18,12},{20,14},{22,16},{... | collective-permute-start | bytes 1572872 | tf_op jit(solution)/shard_map/ppermute | solution.py:13
  113.1 43.2 %collective-permute-start.10 = (bf16[256,8,128]{2,0,1:T(8,128)(2,1)}, bf16[256,8,128]{2,0,1:T(8,128)(2,1)}, u32[]{:S(2)}, u32[]{:S(2)}) collective-permute-start(bf16[256,8,128]{2,0,1:T(8,128)(2,1)} %get-tuple-element.18), channel_id=1, source_target_pairs={{4,0},{6,2},{8,4},{10,6},{12,8},{14,10},{16,12},{18,14},{20,16},{2... | collective-permute-start | bytes 1572872 | tf_op jit(solution)/shard_map/ppermute | solution.py:13
  116.6 16.1 %all-to-all-start.3 = ((bf16[256,8,128]{2,1,0:T(8,128)(2,1)}), bf16[256,8,128]{2,1,0:T(8,128)(2,1)S(1)}, u32[]{:S(2)}, u32[]{:S(2)}) async-start(bf16[256,8,128]{2,1,0:T(8,128)(2,1)} %copy.51), calls=%async_computation.3 | async-start | bytes 1048576 | tf_op jit(solution)/shard_map/all_to_all | solution.py:105
  132.6 26.6 %all-to-all-start.6 = ((bf16[256,8,128]{2,1,0:T(8,128)(2,1)}), bf16[256,8,128]{2,1,0:T(8,128)(2,1)S(1)}, u32[]{:S(2)}, u32[]{:S(2)}) async-start(bf16[256,8,128]{2,1,0:T(8,128)(2,1)} %copy.59), calls=%async_computation.6 | async-start | bytes 1048576 | tf_op jit(solution)/shard_map/all_to_all | solution.py:112
  138.0 18.3 %copy-start.6 = (bf16[256,8,128]{2,0,1:T(8,128)(2,1)}, bf16[256,8,128]{2,0,1:T(8,128)(2,1)S(1)}, u32[]{:S(2)}) copy-start(bf16[256,8,128]{2,0,1:T(8,128)(2,1)S(1)} %collective-permute-done.11) | copy-start | bytes 1572868
  159.2 10.1 %all-to-all-start.7 = ((bf16[256,8,128]{2,1,0:T(8,128)(2,1)}), bf16[256,8,128]{2,1,0:T(8,128)(2,1)S(1)}, u32[]{:S(2)}, u32[]{:S(2)}) async-start(bf16[256,8,128]{2,1,0:T(8,128)(2,1)} %copy.62), calls=%async_computation.7 | async-start | bytes 1048576 | tf_op jit(solution)/shard_map/all_to_all | solution.py:115
